TPU v7x, 512 devices: a whole 4x4x16 slice. The times are simulated.
512 devices in a mesh: ctx: 64 (over y, z_lo, core), tp: 8 (over z_hi, x).
Axes of the slice: x: 4, y: 4, z: 16 (z_hi: 2, z_lo: 8; z = z_hi * 8 + z_lo), core: 2. Of those that a mesh axis runs over, the one named last changes fastest.
Arguments:
- qkv_values: bfloat16 [16384, 3, 8192], P('ctx', None, 'tp'), may hold values from -6 to 6
- short_taps: float32 [7, 3, 8192], P(None, None, 'tp'), may hold values from -2 to 2
- medium_taps: float32 [128, 8192], P(None, 'tp'), may hold values from -0.5 to 0.5
- skip_gain: float32 [8192], P('tp'), may hold values from -4 to 4
- out_weight: bfloat16 [8192, 4096], P('tp', 'ctx'), may hold values from -0.0625 to 0.0625
Outputs:
- block_out: bfloat16 [16384, 4096], P('ctx', 'tp')
All inputs are finite; a program needn't handle non-finite values.
Results may differ from a plain program's by a relative error of at most 0.015.
Values may be sent and summed in bfloat16 or wider, within the bound.
A program may use at most 64 MiB of HBM per device.

v0:
```python
import jax
import jax.numpy as jnp
from jax import lax
from jax.sharding import PartitionSpec as P


def shifted(value, axis, steps):
    count = lax.axis_size(axis)
    first, last = (max(0, -steps), min(count, count - steps))
    return lax.ppermute(value, axis, [(source, source + steps) for source in range(first, last)])


def causal_taps(extended, tap_table, length):
    tap_count = tap_table.shape[0]
    first_row = extended.shape[0] - length
    summed = jnp.zeros((length,) + extended.shape[1:], jnp.float32)
    for offset in range(tap_count):
        window = lax.slice_in_dim(extended, first_row - offset, first_row - offset + length, axis=0)
        summed = summed + tap_table[offset] * window.astype(jnp.float32)
    return summed


def on_device(qkv_values, short_taps, medium_taps, skip_gain, out_weight):
    tokens_here = qkv_values.shape[0]
    short_reach = short_taps.shape[0] - 1
    medium_reach = medium_taps.shape[0] - 1
    before = shifted(qkv_values[tokens_here - short_reach :], "ctx", 1)
    extended = jnp.concatenate([before, qkv_values], axis=0)
    shortened = causal_taps(extended, short_taps, tokens_here)
    queries = shortened[:, 0]
    product = shortened[:, 1] * shortened[:, 2]
    earlier = shifted(product[tokens_here - medium_reach :], "ctx", 1)
    product_ext = jnp.concatenate([earlier, product], axis=0)
    carried = causal_taps(product_ext, medium_taps, tokens_here)
    gated_out = (queries * (carried + skip_gain * product)).astype(jnp.bfloat16)
    partials = jnp.dot(
        gated_out,
        lax.all_gather(out_weight, "ctx", axis=1, tiled=True),
        preferred_element_type=jnp.float32,
    )
    summed = lax.psum_scatter(partials.astype(jnp.bfloat16), "tp", scatter_dimension=1, tiled=True)
    return summed


def solution(mesh):
    return jax.shard_map(
        on_device,
        mesh=mesh,
        in_specs=(
            P("ctx", None, "tp"),
            P(None, None, "tp"),
            P(None, "tp"),
            P("tp"),
            P("tp", "ctx"),
        ),
        out_specs=P("ctx", "tp"),
        check_vma=False,
    )
```

profile of v0, /device:TPU:8, one launch (start us, length us, event | category | flops | bytes accessed | tf_op | source)
XLA Modules:
  0.0 304.1 jit_solution(7082663197515116327)
XLA Ops:
  6.5 0.0 all-gather.2.cloned.1.call-start
  6.5 0.7 all-gather.2.cloned.1.call-update
  7.3 0.0 reduce-scatter.2.cloned.1.call-start
  7.3 0.8 slice.824
  8.1 1.9 collective-permute-start
  10.0 1.3 fusion.397
  11.4 1.1 fusion.396
  12.6 1.4 fusion.391
  14.0 1.4 fusion.390
  15.4 1.4 fusion.395
  16.8 5.6 %collective-permute-done = bf16[6,3,1024]{2,0,1:T(8,128)(2,1)S(1)} collective-permute-done((bf16[6,3,1024]{2,0,1:T(8,128)(2,1)S(1)}, bf16[6,3,1024]{2,0,1:T(8,128)(2,1)S(1)}, u32[]{:S(2)}, u32[]{:S(2)}) %collective-permute-start) | collective-permute-done | bytes 36896 | tf_op jit(solution)/shard_map/ppermute | solution.py:10
  22.4 7.1 %multiply_add_fusion = f32[256,3,1024]{2,0,1:T(8,128)S(1)} fusion(bf16[256,3,1024]{2,0,1:T(8,128)(2,1)} %param.5, bf16[6,3,1024]{2,0,1:T(8,128)(2,1)S(1)} %collective-permute-done, f32[3,1024]{1,0:T(4,128)S(1)} %get-tuple-element.142, f32[3,1024]{1,0:T(4,128)S(1)} %get-tuple-element.143, f32[3,1024]{1,0:T(4,128)S(1)} %get-tuple-element.144, ...), kind=kLoop, calls=%fused_computation.258 | loop fusion | flops 29884416 | bytes 4841472 | tf_op jit(solution)/shard_map/add | solution.py:19
  29.5 0.0 copy-start
  29.5 0.3 broadcast_multiply_fusion
  29.8 1.9 collective-permute-start.1
  31.8 1.3 fusion.394
  33.1 1.4 fusion.393
  34.5 1.4 fusion.392
  35.9 16.9 %collective-permute-done.1 = f32[127,1024]{1,0:T(8,128)S(1)} collective-permute-done((f32[127,1024]{1,0:T(8,128)S(1)}, f32[127,1024]{1,0:T(8,128)S(1)}, u32[]{:S(2)}, u32[]{:S(2)}) %collective-permute-start.1) | collective-permute-done | bytes 520224 | tf_op jit(solution)/shard_map/ppermute | solution.py:10
  52.8 0.0 copy-done
  52.8 26.8 %fusion.487 = bf16[256,1024]{1,0:T(8,128)(2,1)S(1)} fusion(f32[256,1024]{1,0:T(8,128)S(1)} %bitcast.158, f32[127,1024]{1,0:T(8,128)S(1)} %collective-permute-done.1, f32[256,3,1024]{2,0,1:T(8,128)S(1)} %multiply_add_fusion, f32[1024]{0:T(1024)S(1)} %copy-done, f32[1024]{0:T(1024)S(1)} %bitcast.171, f32[1024]{0:T(1024)S(1)} %bitcast.172, ...), kind=kLoop, calls=%fused_computation.274.clone.clone.1 | loop fusion | flops 100925440 | bytes 4714496 | tf_op jit(solution)/shard_map/dot_general | solution.py:36
  79.6 62.6 %all-gather.2.cloned.1.call-done = bf16[1024,4096]{0,1:T(8,128)(2,1)} async-done(((bf16[1024,64]{0,1:T(8,128)(2,1)}), bf16[1024,4096]{0,1:T(8,128)(2,1)}) %all-gather.2.cloned.1.call-update) | async-done | bytes 8388624 | tf_op jit(solution)/shard_map/all_gather | solution.py:38
  142.3 7.1 %convolution_convert_fusion = bf16[256,4096]{1,0:T(8,128)(2,1)} fusion(bf16[1024,4096]{0,1:T(8,128)(2,1)} %all-gather.2.cloned.1.call-done, bf16[256,1024]{1,0:T(8,128)(2,1)S(1)} %fusion.487), kind=kOutput, calls=%fused_computation.252 | convolution fusion | flops 2148532224 | bytes 11010048 | tf_op jit(solution)/shard_map/dot_general | solution.py:36
  149.4 0.0 reduce-scatter.2.cloned.1.call-update
  149.4 147.8 %reduce-scatter.2.cloned.1.call-done = bf16[256,512]{1,0:T(8,128)(2,1)} async-done(((bf16[256,4096]{1,0:T(8,128)(2,1)}), bf16[256,512]{1,0:T(8,128)(2,1)}) %reduce-scatter.2.cloned.1.call-update) | async-done | bytes 262160 | tf_op jit(solution)/shard_map/reduce_scatter | solution.py:41
  (5 shorter events, 0.1 us)
Async XLA Ops:
  6.5 135.7 %all-gather.2.cloned.1.call-start = ((), (), s32[]{:S(2)}) async-start(), calls=%async_computation.1 | async-start | bytes 8519680 | tf_op jit(solution)/shard_map/all_gather | solution.py:38
  7.3 290.0 %reduce-scatter.2.cloned.1.call-start = ((), (), s32[]{:S(2)}) async-start(), calls=%async_computation.2 | async-start | bytes 2359296 | tf_op jit(solution)/shard_map/reduce_scatter | solution.py:41
  8.1 14.3 %collective-permute-start = (bf16[6,3,1024]{2,0,1:T(8,128)(2,1)S(1)}, bf16[6,3,1024]{2,0,1:T(8,128)(2,1)S(1)}, u32[]{:S(2)}, u32[]{:S(2)}) collective-permute-start(bf16[6,3,1024]{2,0,1:T(8,128)(2,1)S(1)} %slice.824), channel_id=1, source_target_pairs={{0,8},{8,16},{16,24},{24,32},{32,40},{40,48},{48,56},{56,64},{64,7... | collective-permute-start | bytes 110600 | tf_op jit(solution)/shard_map/ppermute | solution.py:10
  29.5 23.3 %copy-start = (f32[1024]{0:T(1024)S(1)}, f32[1024]{0:T(1024)}, u32[]{:S(2)}) copy-start(f32[1024]{0:T(1024)} %param.8) | copy-start | bytes 12292
  29.8 22.9 %collective-permute-start.1 = (f32[127,1024]{1,0:T(8,128)S(1)}, f32[127,1024]{1,0:T(8,128)S(1)}, u32[]{:S(2)}, u32[]{:S(2)}) collective-permute-start(f32[127,1024]{1,0:T(8,128)S(1)} %slice_bitcast_fusion.1), channel_id=1, source_target_pairs={{0,8},{8,16},{16,24},{24,32},{32,40},{40,48},{48,56},{56,64},{64,7... | collective-permute-start | bytes 1560584 | tf_op jit(solution)/shard_map/ppermute | solution.py:10
Sparse Core Ops, SparseCore 0:
  9.5 132.7 all-gather.1
  149.5 147.6 reduce-scatter.1
where the time goes:
time: 305 us; the launch traced here: 304 us
  waiting for transfers between devices  234 us (77%)
  other arithmetic  34.2 us (11%)
  between operations  13.5 us (4%)
  local copies, waits for them, and re-layouts  11.6 us (4%)
  matrix products  7.14 us (2%)
  starting transfers between devices  3.88 us (1%)
    reduce_scatter x1, waiting for transfers between devices, on_device(): lax.psum_scatter(partials.astype(jnp.bfloat16), 'tp', scatter_dimension=1...  148 us
    all_gather x1, waiting for transfers between devices, on_device(): lax.all_gather(out_weight, 'ctx', axis=1, tiled=True)  62.6 us
    dot_general x1, other arithmetic, on_device(): jnp.dot(gated_out, lax.all_gather(out_weight, 'ctx', axis=1, tiled=True),...  26.8 us
    ppermute x2, waiting for transfers between devices, shifted(): lax.ppermute(value, axis, [(source, source + steps) for source in range(f...  22.5 us
    slice x8, local copies, waits for them, and re-layouts, causal_taps(): summed = summed + tap_table[offset] * window.astype(jnp.float32)  10.7 us
    dot_general x1, matrix products, on_device(): jnp.dot(gated_out, lax.all_gather(out_weight, 'ctx', axis=1, tiled=True),...  7.14 us
    add x1, other arithmetic, causal_taps(): summed = summed + tap_table[offset] * window.astype(jnp.float32)  7.09 us
  transfers between devices with their start and end apart: 4, of which 4 were waited for; matrix products, arithmetic and copies ran while one was open for 15% of the time, Pallas kernels for 0%

commit v1 on v0

v1 whole, which is shorter than its diff:
```python
import numpy as np
import jax
import jax.numpy as jnp
from jax import lax
from jax.experimental import pallas as pl
from jax.experimental.pallas import tpu as pltpu
from jax.sharding import PartitionSpec as P

MESH = pl.DeviceIdType.MESH
F32, BF16 = jnp.float32, jnp.bfloat16
NT = (((1,), (1,)), ((), ()))


def dft_tables():
    n = np.arange(256)
    k = np.arange(128)[:, None]
    angle = 2 * np.pi * ((k * n) % 256) / 256
    imag = -np.sin(angle)
    imag[0] = 1 - 2 * (n % 2)
    forward = np.concatenate([np.cos(angle), imag], axis=0)
    weight = np.full((256, 1), 2 / 256)
    weight[0] = weight[128] = 1 / 256
    inverse = (forward * weight).T[128:]

    def split(table):
        high = table.astype(jnp.bfloat16)
        return np.stack([high, (table - high.astype(np.float64)).astype(jnp.bfloat16)])

    return split(forward), split(inverse)


def dot(a, b):
    return jnp.dot(a, b, preferred_element_type=F32)


def kernel(q_hbm, st_hbm, mt_hbm, gain_hbm, w_hbm, f_hbm, i_hbm, out_ref,
           qv, st, mt, gain, fwd, inv, halo, streams, prod, px, query, spec, gated,
           wbuf, pb, xr, fin, zs_buf, zr_buf,
           load_sem, halo_send, halo_recv, wr, s_z, s_y, s_f, s_p, x_send, x_recv, zx_send, zx_recv):
    ctx, tp = lax.axis_index("ctx"), lax.axis_index("tp")
    y, z, c = ctx // 16, (ctx // 2) % 8, ctx % 2
    zh, x = tp // 4, tp % 4

    def dev(yy, zz, cc):
        return {"ctx": (yy * 8 + zz) * 2 + cc, "tp": tp}

    y_next, y_prev, y_far = (y + 1) % 4, (y + 3) % 4, (y + 2) % 4
    other_half = {"ctx": ctx, "tp": (1 - zh) * 4 + x}

    def block_index(ys, zs, cc):
        return (ys * 8 + zs) * 2 + cc

    def rows_of(b):
        return pl.ds(pl.multiple_of(b * 64, 64), 64)

    own = block_index(y, z, c)
    loads = [
        pltpu.make_async_copy(w_hbm, wbuf.at[rows_of(own)], load_sem.at[0]),
        pltpu.make_async_copy(q_hbm, qv, load_sem.at[1]),
        pltpu.make_async_copy(st_hbm, st, load_sem.at[2]),
        pltpu.make_async_copy(mt_hbm, mt, load_sem.at[3]),
        pltpu.make_async_copy(gain_hbm, gain, load_sem.at[4]),
        pltpu.make_async_copy(f_hbm, fwd, load_sem.at[5]),
        pltpu.make_async_copy(i_hbm, inv, load_sem.at[6]),
    ]
    for load in loads:
        load.start()

    barrier = pltpu.get_barrier_semaphore()

    def greet(target):
        pl.semaphore_signal(barrier, inc=1, device_id=target, device_id_type=MESH)

    greet(other_half)
    pl.when(ctx > 0)(lambda: greet({"ctx": ctx - 1, "tp": tp}))
    pl.when(z > 0)(lambda: greet(dev(y, z - 1, c)))
    pl.when(z < 7)(lambda: greet(dev(y, z + 1, c)))
    greet(dev(y_next, z, c))
    greet(dev(y_prev, z, c))
    for step in range(1, 4):
        greet({"ctx": ctx, "tp": zh * 4 + (x + step) % 4})
    greet(dev(y, z, 1 - c))
    loads[0].wait()
    loads[1].wait()
    pl.semaphore_wait(barrier, 7 + (1 - z // 7) + (z + 7) // 8 + (1 - ctx // 63))

    def remote(src, dst, send, recv, target):
        return pltpu.make_async_remote_copy(
            src_ref=src, dst_ref=dst, send_sem=send, recv_sem=recv, device_id=target, device_id_type=MESH)

    def block_copy(b, send, target, half=0, piece=None):
        rows = rows_of(b) if piece is None else pl.ds(pl.multiple_of(b * 64 + piece * 32, 32), 32)
        return remote(wbuf.at[rows], wbuf.at[rows], send, wr.at[b, half], target)

    def z_up(zs):
        return block_copy(block_index(y, zs, c), s_z.at[0, zs], dev(y, z + 1, c))

    def z_down(zs):
        return block_copy(block_index(y, zs, c), s_z.at[1, zs], dev(y, z - 1, c))

    def y_up(zs):
        return block_copy(block_index(y, zs, c), s_y.at[0, zs], dev(y_next, z, c))

    def y_down(zs):
        return block_copy(block_index(y, zs, c), s_y.at[1, zs], dev(y_prev, z, c))

    def y_on_up(zs):
        return block_copy(block_index(y_prev, zs, c), s_f.at[0, zs], dev(y_next, z, c), 0, 0)

    def y_on_down(zs):
        return block_copy(block_index(y_next, zs, c), s_f.at[1, zs], dev(y_prev, z, c), 1, 1)

    def to_partner(ys, zs):
        return block_copy(block_index(ys, zs, c), s_p.at[ys, zs], dev(y, z, 1 - c))

    def arrived(b, half=0, piece=None):
        block_copy(b, s_p.at[0, 0], dev(y, z, 1 - c), half, piece).wait_recv()

    low = 1 - z // 4
    near = z * low + (7 - z) * (1 - low)

    def place(k):
        far = (k - 2 * near + 15) // 16
        return z + (1 - far) * ((k + 1) // 2) * (1 - 2 * ((k + 1) % 2)) + far * (k - near) * (2 * low - 1)

    def step_z(k, first=False):
        zs = z if first else place(k)
        if not first:
            arrived(block_index(y, zs, c))
        pl.when((zs <= z) & (z < 7))(lambda: z_up(zs).start())
        pl.when((zs >= z) & (z > 0))(lambda: z_down(zs).start())
        y_up(zs).start()
        y_down(zs).start()
        to_partner(y, zs).start()

    def step_y(k):
        zs = place(k)
        arrived(block_index(y_prev, zs, c))
        y_on_up(zs).start()
        to_partner(y_prev, zs).start()
        arrived(block_index(y_next, zs, c))
        y_on_down(zs).start()
        to_partner(y_next, zs).start()

    def step_y_far(k):
        zs = place(k)
        arrived(block_index(y_far, zs, c), 0, 0)
        arrived(block_index(y_far, zs, c), 1, 1)
        to_partner(y_far, zs).start()

    def x_copy(owner, slot):
        return remote(pb.at[owner, slot], xr.at[(x - owner + 4) % 4 - 1, slot], x_send.at[owner, slot],
                      x_recv.at[(x - owner + 4) % 4 - 1, slot], {"ctx": ctx, "tp": zh * 4 + owner})

    def z_copy(i):
        return remote(zs_buf.at[i], zr_buf.at[i], zx_send.at[i], zx_recv.at[i], other_half)

    def unit(k, dy):
        zs, ys = place(k), (y + dy) % 4
        arrived(block_index(ys, zs, 1 - c))
        block = wbuf[pl.ds(pl.multiple_of((ys * 8 + zs) * 128, 128), 128), :]
        part = lax.dot_general(gated[...], block, NT, preferred_element_type=F32)
        owner, slot = (ys % 2) * 2 + zs // 4, (ys // 2) * 4 + zs % 4
        pb[owner, slot] = part.astype(BF16)
        pl.when(owner != x)(lambda: x_copy(owner, slot).start())

    def gather_sum(k, dy):
        zs, ys = place(k), (y + dy) % 4
        owner, slot, i = (ys % 2) * 2 + zs // 4, (ys // 2) * 4 + zs % 4, zs % 4

        @pl.when(owner == x)
        def _():
            for s in range(3):
                remote(pb.at[0, 0], xr.at[s, slot], x_send.at[0, 0], x_recv.at[s, slot], other_half).wait_recv()
            total = pb[x, slot].astype(F32)
            for s in range(3):
                total = total + xr[s, slot].astype(F32)

            @pl.when(ys // 2 == zh)
            def _():
                fin[i] = total

            @pl.when(ys // 2 != zh)
            def _():
                zs_buf[i] = total.astype(BF16)
                z_copy(i).start()

    step_z(0, first=True)

    following = {"ctx": ctx + 1, "tp": tp}
    tail_copy = remote(qv.at[:, pl.ds(240, 16), :], halo, halo_send.at[0], halo_recv.at[0], following)
    prod_copy = remote(px.at[pl.ds(256, 128)], px.at[pl.ds(0, 128)], halo_send.at[1], halo_recv.at[1], following)
    pl.when(ctx < 63)(lambda: tail_copy.start())
    loads[2].wait()

    def lanes(ch, width=128):
        return pl.ds(pl.multiple_of(ch * width, width), width)

    def short(i, ch, first, count):
        total = None
        for j in range(7):
            term = st[i, j:j + 1, lanes(ch)] * streams[i, ch, pl.ds(16 + first - j, count), :]
            total = term if total is None else total + term
        return total

    def conv_late(ch, carry):
        for i in (1, 2):
            streams[i, ch, 16:272, :] = qv[i, :, lanes(ch)].astype(F32)
        value = short(1, ch, 128, 128) * short(2, ch, 128, 128)
        prod[128:256, lanes(ch)] = value
        px[256:384, lanes(ch)] = value.astype(BF16)
        return carry

    lax.fori_loop(0, 8, conv_late, 0)
    pl.when(ctx < 63)(lambda: prod_copy.start())

    step_z(1)

    @pl.when(ctx > 0)
    def _():
        tail_copy.wait_recv()

    @pl.when(ctx == 0)
    def _():
        halo[...] = jnp.zeros_like(halo)
        px[0:128, :] = jnp.zeros((128, 1024), BF16)

    def conv_early(ch, carry):
        for i in range(3):
            streams[i, ch, 0:16, :] = halo[i, :, lanes(ch)].astype(F32)
        streams[0, ch, 16:272, :] = qv[0, :, lanes(ch)].astype(F32)
        value = short(1, ch, 0, 128) * short(2, ch, 0, 128)
        prod[0:128, lanes(ch)] = value
        px[128:256, lanes(ch)] = value.astype(BF16)
        query[0:128, lanes(ch)] = short(0, ch, 0, 128)
        query[128:256, lanes(ch)] = short(0, ch, 128, 128)
        return carry

    lax.fori_loop(0, 8, conv_early, 0)
    step_z(2)
    step_y(0)

    for load in loads[3:]:
        load.wait()
    pl.when(ctx > 0)(lambda: prod_copy.wait_recv())

    def medium(group, carry):
        at = lanes(group, 256)
        taps = mt[:, at]
        taps_high = taps.astype(BF16)
        taps_low = (taps - taps_high.astype(F32)).astype(BF16)
        spectrum = (dot(fwd[0, :, 0:128], taps_high) + dot(fwd[0, :, 0:128], taps_low)
                    + dot(fwd[1, :, 0:128], taps_high))
        first = lax.broadcasted_iota(jnp.int32, (128, 256), 0) == 0
        h_real, h_imag = spectrum[0:128], spectrum[128:256]
        h_cross = jnp.where(first, 0.0, h_imag)
        h_last = jnp.where(first, h_imag, h_real)
        for part in range(2):
            seg = px[128 * part:128 * part + 256, at]
            x_all = dot(fwd[0], seg) + dot(fwd[1], seg)
            x_real, x_imag = x_all[0:128], x_all[128:256]
            spec[0:128, :] = x_real * h_real - x_imag * h_cross
            spec[128:256, :] = x_real * h_cross + x_imag * h_last
            whole = spec[...]
            high = whole.astype(BF16)
            low_part = (whole - high.astype(F32)).astype(BF16)
            carried = dot(inv[0], high) + dot(inv[0], low_part) + dot(inv[1], high)
            here = slice(128 * part, 128 * part + 128)
            gated[here, at] = (query[here, at] * (carried + gain[0:1, at] * prod[here, at])).astype(BF16)
        return carry

    lax.fori_loop(0, 4, medium, 0)

    def main(t, carry):
        pl.when(t < 8)(lambda: step_z(t))
        pl.when(t < 10)(lambda: step_y(t - 2))
        pl.when(t < 11)(lambda: step_y_far(t - 3))

        @pl.when(t < 11)
        def _():
            for dy in (0, 1, 3):
                unit(t - 3, dy)

        @pl.when((t >= 4) & (t < 12))
        def _():
            unit(t - 4, 2)
            for dy in (0, 1, 3):
                gather_sum(t - 4, dy)

        @pl.when(t >= 5)
        def _():
            gather_sum(t - 5, 2)

        return carry

    lax.fori_loop(3, 13, main, 0)

    for i in range(4):
        z_copy(i).wait_recv()
        out_ref[:, 128 * i:128 * i + 128] = (fin[i] + zr_buf[i].astype(F32)).astype(BF16)

    def drain(zs, carry):
        pl.when((zs <= z) & (z < 7))(lambda: z_up(zs).wait_send())
        pl.when((zs >= z) & (z > 0))(lambda: z_down(zs).wait_send())
        for copy in (y_up, y_down, y_on_up, y_on_down):
            copy(zs).wait_send()
        for ys in range(4):
            to_partner(ys, zs).wait_send()
        for step in range(1, 4):
            x_copy((x + step) % 4, zs).wait_send()
        return carry

    lax.fori_loop(0, 8, drain, 0)
    for i in range(4):
        z_copy(i).wait_send()

    @pl.when(ctx < 63)
    def _():
        tail_copy.wait_send()
        prod_copy.wait_send()


def on_device(qkv_values, short_taps, medium_taps, skip_gain, out_weight):
    forward, inverse = dft_tables()
    dma = pltpu.SemaphoreType.DMA
    return pl.pallas_call(
        kernel,
        out_shape=jax.ShapeDtypeStruct((256, 512), BF16),
        in_specs=[pl.BlockSpec(memory_space=pl.ANY)] * 7,
        out_specs=pl.BlockSpec(memory_space=pltpu.VMEM),
        scratch_shapes=[
            pltpu.VMEM((3, 256, 1024), BF16),
            pltpu.VMEM((3, 7, 1024), F32),
            pltpu.VMEM((128, 1024), F32),
            pltpu.VMEM((1, 1024), F32),
            pltpu.VMEM((2, 256, 256), BF16),
            pltpu.VMEM((2, 128, 256), BF16),
            pltpu.VMEM((3, 16, 1024), BF16),
            pltpu.VMEM((3, 8, 272, 128), F32),
            pltpu.VMEM((256, 1024), F32),
            pltpu.VMEM((384, 1024), BF16),
            pltpu.VMEM((256, 1024), F32),
            pltpu.VMEM((256, 256), F32),
            pltpu.VMEM((256, 1024), BF16),
            pltpu.VMEM((4096, 1024), BF16),
            pltpu.VMEM((4, 8, 256, 128), BF16),
            pltpu.VMEM((3, 8, 256, 128), BF16),
            pltpu.VMEM((4, 256, 128), F32),
            pltpu.VMEM((4, 256, 128), BF16),
            pltpu.VMEM((4, 256, 128), BF16),
            dma((7,)),
            dma((2,)), dma((2,)),
            dma((64, 2)),
            dma((2, 8)), dma((2, 8)), dma((2, 8)), dma((4, 8)),
            dma((4, 8)), dma((3, 8)),
            dma((4,)), dma((4,)),
        ],
        compiler_params=pltpu.CompilerParams(
            collective_id=0, has_side_effects=True, vmem_limit_bytes=48 * 2**20),
        cost_estimate=pl.CostEstimate(flops=3 * 10**9, bytes_accessed=4 * 10**6, transcendentals=0),
    )(
        jnp.transpose(qkv_values, (1, 0, 2)),
        jnp.transpose(short_taps, (1, 0, 2)),
        medium_taps,
        skip_gain.reshape(1, -1),
        out_weight.T,
        jnp.asarray(forward),
        jnp.asarray(inverse),
    )


def solution(mesh):
    return jax.shard_map(
        on_device,
        mesh=mesh,
        in_specs=(
            P("ctx", None, "tp"),
            P(None, None, "tp"),
            P(None, "tp"),
            P("tp"),
            P("tp", "ctx"),
        ),
        out_specs=P("ctx", "tp"),
        check_vma=False,
    )
```

time: 305 us -> 106 us (0.35)
  the two profiles are of different devices: /device:TPU:8 before, /device:TPU:480 now
where the time goes in v1:
time: 106 us; the launch traced here: 105 us
  Pallas kernels  97.8 us (92%)
  local copies, waits for them, and re-layouts  7.49 us (7%)
    pallas_call x1, Pallas kernels, on_device(): pl.pallas_call(kernel, out_shape=jax.ShapeDtypeStruct((256, 512), BF16),...  97.8 us
    unnamed x15, local copies, waits for them, and re-layouts  7.49 us

profile of v1, /device:TPU:480, one launch (start us, length us, event | category | flops | bytes accessed | tf_op | source)
XLA Modules:
  0.0 105.3 jit_solution(4404073307502057437)
XLA Ops:
  0.0 0.0 copy-start
  0.0 1.4 %copy-done = bf16[256,3,1024]{2,0,1:T(8,128)(2,1)S(1)} copy-done((bf16[256,3,1024]{2,0,1:T(8,128)(2,1)S(1)}, bf16[256,3,1024]{2,0,1:T(8,128)(2,1)}, u32[]{:S(2)}) %copy-start) | copy-done | bytes 1572888
  1.4 0.0 copy-start.1
  1.4 1.0 copy-done.1
  2.5 0.0 copy-start.2
  2.5 0.9 copy-done.2
  3.4 0.0 copy-start.3
  3.4 0.9 copy-done.3
  4.2 0.0 copy-start.4
  4.3 0.7 copy-done.4
  4.9 0.0 copy-start.5
  4.9 0.9 copy-done.5
  5.9 0.0 copy-start.6
  5.9 0.9 copy-done.6
  6.8 97.8 %shard_map.73 = bf16[256,512]{1,0:T(8,128)(2,1)S(1)} custom-call(bf16[3,256,1024]{2,1,0:T(8,128)(2,1)S(1)} %bitcast.4, f32[3,7,1024]{2,1,0:T(8,128)S(1)} %bitcast.6, f32[128,1024]{1,0:T(8,128)S(1)} %copy-done.1, f32[1,1024]{1,0:T(1,128)S(1)} %bitcast.7, bf16[64,1024]{1,0:T(8,128)(2,1)S(1)} %bitcast.5, bf16[2,256,256]{2,1,0:T(8,128)(2,1)S(1)} %copy-done.5, ...), custom_call_target="tpu_custom_call" | custom-call | flops 3000000000 | bytes 4000000 | tf_op jit(solution)/shard_map/pallas_call | solution.py:326
  104.6 0.7 copy.9
Async XLA Ops:
  0.0 1.4 %copy-start = (bf16[256,3,1024]{2,0,1:T(8,128)(2,1)S(1)}, bf16[256,3,1024]{2,0,1:T(8,128)(2,1)}, u32[]{:S(2)}) copy-start(bf16[256,3,1024]{2,0,1:T(8,128)(2,1)} %param.7) | copy-start | bytes 4718596
  1.4 1.0 copy-start.1
  2.5 0.9 copy-start.2
  3.4 0.9 copy-start.3
  4.2 0.7 copy-start.4
  4.9 0.9 copy-start.5
  5.9 0.9 copy-start.6

commit v2 on v1

--- a/solution.py
+++ b/solution.py
@@ -35,8 +35,8 @@
 
 def kernel(q_hbm, st_hbm, mt_hbm, gain_hbm, w_hbm, f_hbm, i_hbm, out_ref,
            qv, st, mt, gain, fwd, inv, halo, streams, prod, px, query, spec, gated,
-           wbuf, pb, xr, fin, zs_buf, zr_buf,
-           load_sem, halo_send, halo_recv, wr, s_z, s_y, s_f, s_p, x_send, x_recv, zx_send, zx_recv):
+           wbuf, pb, xf, xr, fin, zs_buf, zr_buf,
+           load_sem, halo_send, halo_recv, wr, s_z, s_y, s_f, s_p, xf_send, xf_recv, xd_send, xd_recv, xl_send, xl_recv, zx_send, zx_recv):
     ctx, tp = lax.axis_index("ctx"), lax.axis_index("tp")
     y, z, c = ctx // 16, (ctx // 2) % 8, ctx % 2
     zh, x = tp // 4, tp % 4
@@ -92,11 +92,11 @@
         rows = rows_of(b) if piece is None else pl.ds(pl.multiple_of(b * 64 + piece * 32, 32), 32)
         return remote(wbuf.at[rows], wbuf.at[rows], send, wr.at[b, half], target)
 
-    def z_up(zs):
-        return block_copy(block_index(y, zs, c), s_z.at[0, zs], dev(y, z + 1, c))
-
-    def z_down(zs):
-        return block_copy(block_index(y, zs, c), s_z.at[1, zs], dev(y, z - 1, c))
+    def z_up(zs, piece):
+        return block_copy(block_index(y, zs, c), s_z.at[0, zs, piece], dev(y, z + 1, c), piece, piece)
+
+    def z_down(zs, piece):
+        return block_copy(block_index(y, zs, c), s_z.at[1, zs, piece], dev(y, z - 1, c), piece, piece)
 
     def y_up(zs):
         return block_copy(block_index(y, zs, c), s_y.at[0, zs], dev(y_next, z, c))
@@ -123,15 +123,27 @@
         far = (k - 2 * near + 15) // 16
         return z + (1 - far) * ((k + 1) // 2) * (1 - 2 * ((k + 1) % 2)) + far * (k - near) * (2 * low - 1)
 
-    def step_z(k, first=False):
-        zs = z if first else place(k)
-        if not first:
-            arrived(block_index(y, zs, c))
-        pl.when((zs <= z) & (z < 7))(lambda: z_up(zs).start())
-        pl.when((zs >= z) & (z > 0))(lambda: z_down(zs).start())
+    def spread(zs):
         y_up(zs).start()
         y_down(zs).start()
         to_partner(y, zs).start()
+
+    def step_z(distance):
+        @pl.when(z >= distance)
+        def _():
+            zs = z - distance
+            for piece in range(2):
+                arrived(block_index(y, zs, c), piece, piece)
+                pl.when(z < 7)(lambda: z_up(zs, piece).start())
+            spread(zs)
+
+        @pl.when(z + distance < 8)
+        def _():
+            zs = z + distance
+            for piece in range(2):
+                arrived(block_index(y, zs, c), piece, piece)
+                pl.when(z > 0)(lambda: z_down(zs, piece).start())
+            spread(zs)
 
     def step_y(k):
         zs = place(k)
@@ -148,9 +160,23 @@
         arrived(block_index(y_far, zs, c), 1, 1)
         to_partner(y_far, zs).start()
 
-    def x_copy(owner, slot):
-        return remote(pb.at[owner, slot], xr.at[(x - owner + 4) % 4 - 1, slot], x_send.at[owner, slot],
-                      x_recv.at[(x - owner + 4) % 4 - 1, slot], {"ctx": ctx, "tp": zh * 4 + owner})
+    def side(slot):
+        return 2 * ((slot // 4 + slot) % 2)
+
+    def along_x(place):
+        return {"ctx": ctx, "tp": zh * 4 + place % 4}
+
+    def far_copy(slot):
+        return remote(pb.at[(x + 2) % 4, slot], xf.at[slot], xf_send.at[slot], xf_recv.at[slot],
+                      along_x(x + 3 + side(slot)))
+
+    def direct_copy(slot):
+        owner = (x + 1 + side(slot)) % 4
+        return remote(pb.at[owner, slot], xr.at[0, slot], xd_send.at[slot], xd_recv.at[slot], along_x(owner))
+
+    def relay_copy(slot):
+        owner = (x + 3 + side(slot)) % 4
+        return remote(pb.at[owner, slot], xr.at[1, slot], xl_send.at[slot], xl_recv.at[slot], along_x(owner))
 
     def z_copy(i):
         return remote(zs_buf.at[i], zr_buf.at[i], zx_send.at[i], zx_recv.at[i], other_half)
@@ -162,7 +188,18 @@
         part = lax.dot_general(gated[...], block, NT, preferred_element_type=F32)
         owner, slot = (ys % 2) * 2 + zs // 4, (ys // 2) * 4 + zs % 4
         pb[owner, slot] = part.astype(BF16)
-        pl.when(owner != x)(lambda: x_copy(owner, slot).start())
+        pl.when(owner == (x + 2) % 4)(lambda: far_copy(slot).start())
+        pl.when(owner == (x + 1 + side(slot)) % 4)(lambda: direct_copy(slot).start())
+
+    def relay(k, dy):
+        zs, ys = place(k), (y + dy) % 4
+        owner, slot = (ys % 2) * 2 + zs // 4, (ys // 2) * 4 + zs % 4
+
+        @pl.when(owner == (x + 3 + side(slot)) % 4)
+        def _():
+            far_copy(slot).wait_recv()
+            pb[owner, slot] = (pb[owner, slot].astype(F32) + xf[slot].astype(F32)).astype(BF16)
+            relay_copy(slot).start()
 
     def gather_sum(k, dy):
         zs, ys = place(k), (y + dy) % 4
@@ -170,11 +207,9 @@
 
         @pl.when(owner == x)
         def _():
-            for s in range(3):
-                remote(pb.at[0, 0], xr.at[s, slot], x_send.at[0, 0], x_recv.at[s, slot], other_half).wait_recv()
-            total = pb[x, slot].astype(F32)
-            for s in range(3):
-                total = total + xr[s, slot].astype(F32)
+            direct_copy(slot).wait_recv()
+            relay_copy(slot).wait_recv()
+            total = pb[x, slot].astype(F32) + xr[0, slot].astype(F32) + xr[1, slot].astype(F32)
 
             @pl.when(ys // 2 == zh)
             def _():
@@ -185,7 +220,10 @@
                 zs_buf[i] = total.astype(BF16)
                 z_copy(i).start()
 
-    step_z(0, first=True)
+    for piece in range(2):
+        pl.when(z < 7)(lambda: z_up(z, piece).start())
+        pl.when(z > 0)(lambda: z_down(z, piece).start())
+    spread(z)
 
     following = {"ctx": ctx + 1, "tp": tp}
     tail_copy = remote(qv.at[:, pl.ds(240, 16), :], halo, halo_send.at[0], halo_recv.at[0], following)
@@ -271,43 +309,46 @@
 
     lax.fori_loop(0, 4, medium, 0)
 
+    def within(t, lag, run):
+        pl.when((t >= lag) & (t < 8 + lag))(lambda: run(t - lag))
+
+    def beside(run):
+        def three(k):
+            for dy in (0, 1, 3):
+                run(k, dy)
+        return three
+
+    def across(run):
+        return lambda k: run(k, 2)
+
     def main(t, carry):
-        pl.when(t < 8)(lambda: step_z(t))
-        pl.when(t < 10)(lambda: step_y(t - 2))
-        pl.when(t < 11)(lambda: step_y_far(t - 3))
-
-        @pl.when(t < 11)
-        def _():
-            for dy in (0, 1, 3):
-                unit(t - 3, dy)
-
-        @pl.when((t >= 4) & (t < 12))
-        def _():
-            unit(t - 4, 2)
-            for dy in (0, 1, 3):
-                gather_sum(t - 4, dy)
-
-        @pl.when(t >= 5)
-        def _():
-            gather_sum(t - 5, 2)
-
+        within(t, 0, step_z)
+        within(t, 2, step_y)
+        within(t, 4, step_y_far)
+        within(t, 3, beside(unit))
+        within(t, 5, beside(relay))
+        within(t, 7, beside(gather_sum))
+        within(t, 5, across(unit))
+        within(t, 7, across(relay))
+        within(t, 9, across(gather_sum))
         return carry
 
-    lax.fori_loop(3, 13, main, 0)
+    lax.fori_loop(3, 17, main, 0)
 
     for i in range(4):
         z_copy(i).wait_recv()
         out_ref[:, 128 * i:128 * i + 128] = (fin[i] + zr_buf[i].astype(F32)).astype(BF16)
 
     def drain(zs, carry):
-        pl.when((zs <= z) & (z < 7))(lambda: z_up(zs).wait_send())
-        pl.when((zs >= z) & (z > 0))(lambda: z_down(zs).wait_send())
+        for piece in range(2):
+            pl.when((zs <= z) & (z < 7))(lambda: z_up(zs, piece).wait_send())
+            pl.when((zs >= z) & (z > 0))(lambda: z_down(zs, piece).wait_send())
         for copy in (y_up, y_down, y_on_up, y_on_down):
             copy(zs).wait_send()
         for ys in range(4):
             to_partner(ys, zs).wait_send()
-        for step in range(1, 4):
-            x_copy((x + step) % 4, zs).wait_send()
+        for copy in (far_copy, direct_copy, relay_copy):
+            copy(zs).wait_send()
         return carry
 
     lax.fori_loop(0, 8, drain, 0)
@@ -344,19 +385,20 @@
             pltpu.VMEM((256, 1024), BF16),
             pltpu.VMEM((4096, 1024), BF16),
             pltpu.VMEM((4, 8, 256, 128), BF16),
-            pltpu.VMEM((3, 8, 256, 128), BF16),
+            pltpu.VMEM((8, 256, 128), BF16),
+            pltpu.VMEM((2, 8, 256, 128), BF16),
             pltpu.VMEM((4, 256, 128), F32),
             pltpu.VMEM((4, 256, 128), BF16),
             pltpu.VMEM((4, 256, 128), BF16),
             dma((7,)),
             dma((2,)), dma((2,)),
             dma((64, 2)),
-            dma((2, 8)), dma((2, 8)), dma((2, 8)), dma((4, 8)),
-            dma((4, 8)), dma((3, 8)),
+            dma((2, 8, 2)), dma((2, 8)), dma((2, 8)), dma((4, 8)),
+            dma((8,)), dma((8,)), dma((8,)), dma((8,)), dma((8,)), dma((8,)),
             dma((4,)), dma((4,)),
         ],
         compiler_params=pltpu.CompilerParams(
-            collective_id=0, has_side_effects=True, vmem_limit_bytes=48 * 2**20),
+            collective_id=0, has_side_effects=True, vmem_limit_bytes=63 * 2**20),
         cost_estimate=pl.CostEstimate(flops=3 * 10**9, bytes_accessed=4 * 10**6, transcendentals=0),
     )(
         jnp.transpose(qkv_values, (1, 0, 2)),

time: 106 us -> 86.7 us (0.82)
  the two profiles are of different devices: /device:TPU:480 before, /device:TPU:385 now
where the time goes in v2:
time: 86.7 us; the launch traced here: 86.4 us
  Pallas kernels  84.7 us (98%)
  local copies, waits for them, and re-layouts  1.67 us (2%)
    pallas_call x1, Pallas kernels, on_device(): pl.pallas_call(kernel, out_shape=jax.ShapeDtypeStruct((256, 512), BF16),...  84.7 us

profile of v2, /device:TPU:385, one launch (start us, length us, event | category | flops | bytes accessed | tf_op | source)
XLA Modules:
  0.0 86.4 jit_solution(3225847846002637529)
XLA Ops:
  0.0 84.7 %shard_map.73 = bf16[256,512]{1,0:T(8,128)(2,1)} custom-call(bf16[3,256,1024]{2,1,0:T(8,128)(2,1)} %bitcast.4, f32[3,7,1024]{2,1,0:T(8,128)} %bitcast.6, f32[128,1024]{1,0:T(8,128)} %mt_hbm.1, f32[1,1024]{1,0:T(1,128)} %bitcast.7, bf16[64,1024]{1,0:T(8,128)(2,1)} %bitcast.5, bf16[2,256,256]{2,1,0:T(8,128)(2,1)} %constant.4.clone.f_hbm, ...), custom_call_target="tpu_custom_call" | custom-call | flops 3000000000 | bytes 4000000 | tf_op jit(solution)/shard_map/pallas_call | solution.py:367
  84.7 1.7 %copy.9 = bf16[256,512]{1,0:T(8,128)(2,1)} copy(bf16[256,512]{1,0:T(8,128)(2,1)} %shard_map.73) | data formatting | bytes 524288

commit v3 on v2

--- a/solution.py
+++ b/solution.py
@@ -277,6 +277,7 @@
     lax.fori_loop(0, 8, conv_early, 0)
     step_z(2)
     step_y(0)
+    step_y(1)
 
     for load in loads[3:]:
         load.wait()
@@ -323,17 +324,20 @@
 
     def main(t, carry):
         within(t, 0, step_z)
-        within(t, 2, step_y)
-        within(t, 4, step_y_far)
-        within(t, 3, beside(unit))
-        within(t, 5, beside(relay))
-        within(t, 7, beside(gather_sum))
-        within(t, 5, across(unit))
-        within(t, 7, across(relay))
-        within(t, 9, across(gather_sum))
+        within(t, 1, step_y)
+        within(t, 3, step_y_far)
+        within(t, 4, beside(relay))
+        within(t, 6, across(relay))
+        within(t, 6, beside(gather_sum))
+        within(t, 8, across(gather_sum))
+        within(t, 2, beside(unit))
+        within(t, 4, across(unit))
         return carry
 
-    lax.fori_loop(3, 17, main, 0)
+    for dy in (0, 1, 3):
+        unit(0, dy)
+
+    lax.fori_loop(3, 16, main, 0)
 
     for i in range(4):
         z_copy(i).wait_recv()

time: 86.7 us -> 85.1 us (0.982)
  Pallas kernels: 84.7 us -> 83.3 us
    pallas_call x1, Pallas kernels: 84.7 us -> 83.3 us  [on_device(): pl.pallas_call(kernel, out_shape=jax.ShapeDtypeStruct((256, 512), BF16),...]
where the time goes in v3:
time: 85.1 us; the launch traced here: 84.9 us
  Pallas kernels  83.3 us (98%)
  local copies, waits for them, and re-layouts  1.67 us (2%)
    pallas_call x1, Pallas kernels, on_device(): pl.pallas_call(kernel, out_shape=jax.ShapeDtypeStruct((256, 512), BF16),...  83.3 us

profile of v3, /device:TPU:385, one launch (start us, length us, event | category | flops | bytes accessed | tf_op | source)
XLA Modules:
  0.0 84.9 jit_solution(3609245936746267206)
XLA Ops:
  0.0 83.3 %shard_map.73 = bf16[256,512]{1,0:T(8,128)(2,1)} custom-call(bf16[3,256,1024]{2,1,0:T(8,128)(2,1)} %bitcast.4, f32[3,7,1024]{2,1,0:T(8,128)} %bitcast.6, f32[128,1024]{1,0:T(8,128)} %mt_hbm.1, f32[1,1024]{1,0:T(1,128)} %bitcast.7, bf16[64,1024]{1,0:T(8,128)(2,1)} %bitcast.5, bf16[2,256,256]{2,1,0:T(8,128)(2,1)} %constant.4.clone.f_hbm, ...), custom_call_target="tpu_custom_call" | custom-call | flops 3000000000 | bytes 4000000 | tf_op jit(solution)/shard_map/pallas_call | solution.py:371
  83.3 1.7 %copy.9 = bf16[256,512]{1,0:T(8,128)(2,1)} copy(bf16[256,512]{1,0:T(8,128)(2,1)} %shard_map.73) | data formatting | bytes 524288

commit v4 on v3

--- a/solution.py
+++ b/solution.py
@@ -326,12 +326,12 @@
         within(t, 0, step_z)
         within(t, 1, step_y)
         within(t, 3, step_y_far)
+        within(t, 8, across(gather_sum))
+        within(t, 6, beside(gather_sum))
+        within(t, 6, across(relay))
         within(t, 4, beside(relay))
-        within(t, 6, across(relay))
-        within(t, 6, beside(gather_sum))
-        within(t, 8, across(gather_sum))
+        within(t, 4, across(unit))
         within(t, 2, beside(unit))
-        within(t, 4, across(unit))
         return carry
 
     for dy in (0, 1, 3):

time: 85.1 us -> 84.2 us (0.989)
  Pallas kernels: 83.3 us -> 82.4 us
    pallas_call x1, Pallas kernels: 83.3 us -> 82.4 us  [on_device(): pl.pallas_call(kernel, out_shape=jax.ShapeDtypeStruct((256, 512), BF16),...]
where the time goes in v4:
time: 84.2 us; the launch traced here: 84.1 us
  Pallas kernels  82.4 us (98%)
  local copies, waits for them, and re-layouts  1.67 us (2%)
    pallas_call x1, Pallas kernels, on_device(): pl.pallas_call(kernel, out_shape=jax.ShapeDtypeStruct((256, 512), BF16),...  82.4 us

profile of v4, /device:TPU:385, one launch (start us, length us, event | category | flops | bytes accessed | tf_op | source)
XLA Modules:
  0.0 84.1 jit_solution(329778250254218444)
XLA Ops:
  0.0 82.4 %shard_map.73 = bf16[256,512]{1,0:T(8,128)(2,1)} custom-call(bf16[3,256,1024]{2,1,0:T(8,128)(2,1)} %bitcast.4, f32[3,7,1024]{2,1,0:T(8,128)} %bitcast.6, f32[128,1024]{1,0:T(8,128)} %mt_hbm.1, f32[1,1024]{1,0:T(1,128)} %bitcast.7, bf16[64,1024]{1,0:T(8,128)(2,1)} %bitcast.5, bf16[2,256,256]{2,1,0:T(8,128)(2,1)} %constant.4.clone.f_hbm, ...), custom_call_target="tpu_custom_call" | custom-call | flops 3000000000 | bytes 4000000 | tf_op jit(solution)/shard_map/pallas_call | solution.py:371
  82.4 1.7 %copy.9 = bf16[256,512]{1,0:T(8,128)(2,1)} copy(bf16[256,512]{1,0:T(8,128)(2,1)} %shard_map.73) | data formatting | bytes 524288

commit v5 on v4

--- a/solution.py
+++ b/solution.py
@@ -324,8 +324,8 @@
 
     def main(t, carry):
         within(t, 0, step_z)
+        within(t, 3, step_y_far)
         within(t, 1, step_y)
-        within(t, 3, step_y_far)
         within(t, 8, across(gather_sum))
         within(t, 6, beside(gather_sum))
         within(t, 6, across(relay))

time: 84.2 us -> 84.3 us (level)
  no operation moved by 1% of the time
where the time goes in v5:
time: 84.3 us; the launch traced here: 84.1 us
  Pallas kernels  82.4 us (98%)
  local copies, waits for them, and re-layouts  1.67 us (2%)
    pallas_call x1, Pallas kernels, on_device(): pl.pallas_call(kernel, out_shape=jax.ShapeDtypeStruct((256, 512), BF16),...  82.4 us

profile of v5, /device:TPU:385, one launch (start us, length us, event | category | flops | bytes accessed | tf_op | source)
XLA Modules:
  0.0 84.1 jit_solution(8063142828055050045)
XLA Ops:
  0.0 82.4 %shard_map.73 = bf16[256,512]{1,0:T(8,128)(2,1)} custom-call(bf16[3,256,1024]{2,1,0:T(8,128)(2,1)} %bitcast.4, f32[3,7,1024]{2,1,0:T(8,128)} %bitcast.6, f32[128,1024]{1,0:T(8,128)} %mt_hbm.1, f32[1,1024]{1,0:T(1,128)} %bitcast.7, bf16[64,1024]{1,0:T(8,128)(2,1)} %bitcast.5, bf16[2,256,256]{2,1,0:T(8,128)(2,1)} %constant.4.clone.f_hbm, ...), custom_call_target="tpu_custom_call" | custom-call | flops 3000000000 | bytes 4000000 | tf_op jit(solution)/shard_map/pallas_call | solution.py:371
  82.4 1.7 %copy.9 = bf16[256,512]{1,0:T(8,128)(2,1)} copy(bf16[256,512]{1,0:T(8,128)(2,1)} %shard_map.73) | data formatting | bytes 524288
